TPU v7x, 32 devices: a whole 2x2x4 slice. The times are simulated.
32 devices in a mesh: row: 4 (over y, x), col: 8 (over z, core).
Axes of the slice: x: 2, y: 2, z: 4, core: 2. Of those that a mesh axis runs over, the one named last changes fastest.
Arguments:
- factors: bfloat16 [10240, 3, 2048], P(('row', 'col')), may hold values from -0.59765625 to 0.59765625
- occ_energy: float32 [300], replicated, may hold values from -3 to -0.5
- vir_energy: float32 [2048], replicated, may hold values from 0.3 to 4
- slab_orbitals: int32 [3], replicated, may hold values from 0 to 299
- pair_list: int32 [16, 2], replicated, may hold values from 0 to 2
- pair_state: int32 [16], replicated, may hold values from 0 to 3
- state_shift: float32 [4], replicated, may hold values from 0.1 to 1
Outputs:
- amplitudes: float32 [16, 2048, 2048], P(None, 'row', 'col')
All inputs are finite; a program needn't handle non-finite values.
Results may differ from a plain program's by a relative error of at most 0.0003.
Values may be sent and summed in bfloat16 or wider, within the bound.
A program may use at most 192 MiB of HBM per device.

v0:
```python
import jax
import jax.numpy as jnp
from jax import lax
from jax.sharding import PartitionSpec as P


def lookup(table, index):
    hits = jnp.arange(table.shape[0], dtype=jnp.int32) == index
    return jnp.sum(jnp.where(hits, table, jnp.zeros_like(table)))


def shards(factors, occ_energy, vir_energy, slab_orbitals, pair_list, pair_state, state_shift):
    n_row = lax.axis_size("row")
    n_col = lax.axis_size("col")
    local_aux, nocc, nvir = factors.shape
    rows_a = nvir // n_row
    cols_b = nvir // n_col
    width = nvir // (n_row * n_col)
    reordered = (
        factors.reshape(local_aux, nocc, n_col, n_row, width)
        .transpose(0, 1, 3, 2, 4)
        .reshape(local_aux, nocc, nvir)
    )
    spread_a, spread_b = (
        lax.all_to_all(factors, ("row", "col"), split_axis=2, concat_axis=0, tiled=True),
        lax.all_to_all(reordered, ("row", "col"), split_axis=2, concat_axis=0, tiled=True),
    )
    block_a = lax.all_gather(spread_a, "col", axis=2, tiled=True)
    block_b = lax.all_gather(spread_b, "row", axis=2, tiled=True)
    contract = (((0,), (0,)), ((), ()))
    orb_axis = block_a.ndim - 2
    vir_a = lax.dynamic_slice_in_dim(vir_energy, lax.axis_index("row") * rows_a, rows_a)
    vir_b = lax.dynamic_slice_in_dim(vir_energy, lax.axis_index("col") * cols_b, cols_b)
    npair = pair_list.shape[0]
    results = []
    for pair in range(npair):
        first = pair_list[pair, 0]
        second = pair_list[pair, 1]
        left = lax.dynamic_index_in_dim(block_a, first, orb_axis, keepdims=False)
        right = lax.dynamic_index_in_dim(block_b, second, orb_axis, keepdims=False)
        kernel = lax.dot_general(left, right, contract, preferred_element_type=jnp.float32)
        e_first = lookup(occ_energy, lookup(slab_orbitals, first))
        e_second = lookup(occ_energy, lookup(slab_orbitals, second))
        shift_value = lookup(state_shift, pair_state[pair])
        denom = vir_a[:, None] + vir_b[None, :] - e_first - e_second + shift_value
        results.append(-kernel / denom)
    return jnp.stack(results)


def solution(mesh):
    placed = (P(("row", "col"), None, None), P(), P(), P(), P(), P(), P())
    return jax.shard_map(
        shards, mesh=mesh, in_specs=placed, out_specs=P(None, "row", "col"), check_vma=False
    )
```

profile of v0, /device:TPU:28, one launch (start us, length us, event | category | flops | bytes accessed | tf_op | source)
XLA Modules:
  0.0 853.0 jit_solution(3476516489133594044)
XLA Ops:
  15.8 31.8 %copy.51 = bf16[320,3,2048]{0,1,2:T(4,128)(2,1)S(1)} copy(bf16[320,3,2048]{0,2,1:T(8,128)(2,1)S(1)} %bitcast.387) | data formatting | bytes 7864320 | tf_op jit(solution)/shard_map/reshape | solution.py:22
  47.6 142.0 %all_to_all.36 = bf16[320,3,2048]{0,1,2:T(4,128)(2,1)S(1)} all-to-all(bf16[320,3,2048]{0,1,2:T(4,128)(2,1)S(1)} %copy.51), channel_id=1, replica_groups=mesh['row'=4,'col'=8] {'row','col'}, dimensions={2} | all-to-all | bytes 7864320 | tf_op jit(solution)/shard_map/all_to_all | solution.py:26
  204.3 10.1 %copy.45 = bf16[320,3,2048]{0,1,2:T(4,128)(2,1)} copy(bf16[320,3,2048]{2,0,1:T(8,128)(2,1)} %param.7) | data formatting | bytes 7864320 | tf_op args[0]
  214.4 143.0 %all_to_all.37 = bf16[320,3,2048]{0,1,2:T(4,128)(2,1)S(1)} all-to-all(bf16[320,3,2048]{0,1,2:T(4,128)(2,1)} %copy.45), channel_id=1, replica_groups=mesh['row'=4,'col'=8] {'row','col'}, dimensions={2} | all-to-all | bytes 7864320 | tf_op jit(solution)/shard_map/all_to_all | solution.py:25
  436.1 10.2 %fusion.302 = (s32[]{:T(128)}, s32[]{:T(128)}, s32[]{:T(128)}, s32[]{:T(128)}, s32[]{:T(128)}, /*index=5*/s32[]{:T(128)}, s32[]{:T(128)}, s32[]{:T(128)}, s32[]{...) fusion(s32[3]{0:T(128)S(1)} %copy-done.3, s32[]{:T(128)} %bitcast.99, ...), kind=kLoop, calls=%fused_computation.366 | loop fusion | flops 120 | bytes 132 | tf_op jit(solution)/shard_map/reduce_sum | solution.py:9
  446.3 9.7 %select_reduce_fusion = (f32[]{:T(128)}, f32[]{:T(128)}, f32[]{:T(128)}, f32[]{:T(128)}, f32[]{:T(128)}, /*index=5*/f32[]{:T(128)}, f32[]{:T(128)}, f32[]{:T(128...) fusion(f32[300]{0:T(512)S(1)} %copy-done.2, s32[]{:T(128)} %get-tuple-element.54, ...), kind=kLoop, calls=%fused_computation.208 | loop fusion | flops 12586 | bytes 1312 | tf_op jit(solution)/shard_map/reduce_sum | solution.py:9
  455.9 10.7 %fusion.303 = (f32[]{:T(128)}, f32[]{:T(128)}, f32[]{:T(128)}, f32[]{:T(128)}, f32[]{:T(128)}, /*index=5*/f32[]{:T(128)}, f32[]{:T(128)}, f32[]{:T(128)}, f32[]{...) fusion(f32[4]{0:T(128)S(1)} %copy-done.4, ...), kind=kLoop, calls=%fused_computation.367 | loop fusion | flops 176 | bytes 144 | tf_op jit(solution)/shard_map/reduce_sum | solution.py:9
  466.7 11.6 %fusion.301 = (s32[]{:T(128)}, s32[]{:T(128)}, s32[]{:T(128)}, s32[]{:T(128)}, s32[]{:T(128)}, /*index=5*/s32[]{:T(128)}, s32[]{:T(128)}, s32[]{:T(128)}, s32[]{...) fusion(s32[3]{0:T(128)S(1)} %copy-done.3, ...), kind=kLoop, calls=%fused_computation.365 | loop fusion | flops 136 | bytes 148 | tf_op jit(solution)/shard_map/reduce_sum | solution.py:9
  478.3 12.0 %select_reduce_fusion.1 = (f32[]{:T(128)}, f32[]{:T(128)}, f32[]{:T(128)}, f32[]{:T(128)}, f32[]{:T(128)}, /*index=5*/f32[]{:T(128)}, f32[]{:T(128)}, f32[]{:T(1...) fusion(f32[300]{0:T(512)S(1)} %copy-done.2, ...), kind=kLoop, calls=%fused_computation.210 | loop fusion | flops 16182 | bytes 1344 | tf_op jit(solution)/shard_map/reduce_sum | solution.py:9
  490.3 199.3 %all-gather.3.cloned.1.call-done = bf16[10240,3,512]{0,2,1:T(8,128)(2,1)} async-done(((bf16[10240,3,64]{0,2,1:T(8,128)(2,1)}), bf16[10240,3,512]{0,2,1:T(8,128)(2,1)}) %all-gather.3.cloned.1.call-update) | async-done | bytes 31457296 | tf_op jit(solution)/shard_map/all_gather | solution.py:28
  689.6 11.7 %fusion.164 = f32[16,512,256]{2,1,0:T(8,128)} fusion(f32[]{:T(128)} %get-tuple-element.83, f32[]{:T(128)} %get-tuple-element.35, f32[]{:T(128)} %get-tuple-element.36, f32[256]{0:T(256)S(1)} %dynamic_slice.107, f32[512]{0:T(512)S(1)} %dynamic_slice.106, bf16[10240,3,256]{0,2,1:T(8,128)(2,1)} %all-gather.5.cloned.1.call-done, s32[]{:T(128)S(6)} %select_n.348, ...), kind=kOutput, calls=%fused_computation.116 | convolution fusion | flops 2685140992 | bytes 16257544 | tf_op jit(solution)/shard_map/dot_general | solution.py:41
  701.3 9.6 %fusion.169 = f32[16,512,256]{2,1,0:T(8,128)} fusion(f32[16,512,256]{2,1,0:T(8,128)} %fusion.164, f32[]{:T(128)} %get-tuple-element.82, f32[]{:T(128)} %get-tuple-element.33, f32[]{:T(128)} %get-tuple-element.34, f32[256]{0:T(256)S(1)} %dynamic_slice.107, f32[512]{0:T(512)S(1)} %dynamic_slice.106, bf16[10240,3,256]{0,2,1:T(8,128)(2,1)S(1)} %copy-done.5, ...), kind=kOutput, calls=%fused_computation.121 | convolution fusion | flops 2685140992 | bytes 16257544 | tf_op jit(solution)/shard_map/dot_general | solution.py:41
  711.0 9.6 %fusion.174 = f32[16,512,256]{2,1,0:T(8,128)} fusion(f32[16,512,256]{2,1,0:T(8,128)} %fusion.169, f32[]{:T(128)} %get-tuple-element.81, f32[]{:T(128)} %get-tuple-element.31, f32[]{:T(128)} %get-tuple-element.32, f32[256]{0:T(256)S(1)} %dynamic_slice.107, f32[512]{0:T(512)S(1)} %dynamic_slice.106, bf16[10240,3,256]{0,2,1:T(8,128)(2,1)S(1)} %copy-done.5, ...), kind=kOutput, calls=%fused_computation.126 | convolution fusion | flops 2685140992 | bytes 16257544 | tf_op jit(solution)/shard_map/dot_general | solution.py:41
  720.6 9.6 %fusion.179 = f32[16,512,256]{2,1,0:T(8,128)} fusion(f32[16,512,256]{2,1,0:T(8,128)} %fusion.174, f32[]{:T(128)} %get-tuple-element.80, f32[]{:T(128)} %get-tuple-element.29, f32[]{:T(128)} %get-tuple-element.30, f32[256]{0:T(256)S(1)} %dynamic_slice.107, f32[512]{0:T(512)S(1)} %dynamic_slice.106, bf16[10240,3,256]{0,2,1:T(8,128)(2,1)S(1)} %copy-done.5, ...), kind=kOutput, calls=%fused_computation.131 | convolution fusion | flops 2685140992 | bytes 16257544 | tf_op jit(solution)/shard_map/dot_general | solution.py:41
  730.2 9.5 %fusion.184 = f32[16,512,256]{2,1,0:T(8,128)} fusion(f32[16,512,256]{2,1,0:T(8,128)} %fusion.179, f32[]{:T(128)} %get-tuple-element.79, f32[]{:T(128)} %get-tuple-element.27, f32[]{:T(128)} %get-tuple-element.28, f32[256]{0:T(256)S(1)} %dynamic_slice.107, f32[512]{0:T(512)S(1)} %dynamic_slice.106, bf16[10240,3,256]{0,2,1:T(8,128)(2,1)S(1)} %copy-done.5, ...), kind=kOutput, calls=%fused_computation.136 | convolution fusion | flops 2685140992 | bytes 16257544 | tf_op jit(solution)/shard_map/dot_general | solution.py:41
  749.3 9.6 %fusion.194 = f32[16,512,256]{2,1,0:T(8,128)} fusion(f32[16,512,256]{2,1,0:T(8,128)} %fusion.189, f32[]{:T(128)} %get-tuple-element.77, f32[]{:T(128)} %get-tuple-element.22, f32[]{:T(128)} %get-tuple-element.24, f32[256]{0:T(256)S(1)} %dynamic_slice.107, f32[512]{0:T(512)S(1)} %dynamic_slice.106, bf16[10240,3,256]{0,2,1:T(8,128)(2,1)S(1)} %copy-done.5, ...), kind=kOutput, calls=%fused_computation.146 | convolution fusion | flops 2685140992 | bytes 16257544 | tf_op jit(solution)/shard_map/dot_general | solution.py:41
  758.8 9.7 %fusion.199 = f32[16,512,256]{2,1,0:T(8,128)} fusion(f32[16,512,256]{2,1,0:T(8,128)} %fusion.194, f32[]{:T(128)} %get-tuple-element.76, f32[]{:T(128)} %get-tuple-element.20, f32[]{:T(128)} %get-tuple-element.21, f32[256]{0:T(256)S(1)} %dynamic_slice.107, f32[512]{0:T(512)S(1)} %dynamic_slice.106, bf16[10240,3,256]{0,2,1:T(8,128)(2,1)S(1)} %copy-done.5, ...), kind=kOutput, calls=%fused_computation.151 | convolution fusion | flops 2685140992 | bytes 16257544 | tf_op jit(solution)/shard_map/dot_general | solution.py:41
  768.5 9.7 %fusion.204 = f32[16,512,256]{2,1,0:T(8,128)} fusion(f32[16,512,256]{2,1,0:T(8,128)} %fusion.199, f32[]{:T(128)} %get-tuple-element.75, f32[]{:T(128)} %get-tuple-element.18, f32[]{:T(128)} %get-tuple-element.19, f32[256]{0:T(256)S(1)} %dynamic_slice.107, f32[512]{0:T(512)S(1)} %dynamic_slice.106, bf16[10240,3,256]{0,2,1:T(8,128)(2,1)S(1)} %copy-done.5, ...), kind=kOutput, calls=%fused_computation.156 | convolution fusion | flops 2685140992 | bytes 16257544 | tf_op jit(solution)/shard_map/dot_general | solution.py:41
  778.2 9.7 %fusion.209 = f32[16,512,256]{2,1,0:T(8,128)} fusion(f32[16,512,256]{2,1,0:T(8,128)} %fusion.204, f32[]{:T(128)} %get-tuple-element.74, f32[]{:T(128)} %get-tuple-element.16, f32[]{:T(128)} %get-tuple-element.17, f32[256]{0:T(256)S(1)} %dynamic_slice.107, f32[512]{0:T(512)S(1)} %dynamic_slice.106, bf16[10240,3,256]{0,2,1:T(8,128)(2,1)S(1)} %copy-done.5, ...), kind=kOutput, calls=%fused_computation.161 | convolution fusion | flops 2685140992 | bytes 16257544 | tf_op jit(solution)/shard_map/dot_general | solution.py:41
  787.9 9.6 %fusion.214 = f32[16,512,256]{2,1,0:T(8,128)} fusion(f32[16,512,256]{2,1,0:T(8,128)} %fusion.209, f32[]{:T(128)} %get-tuple-element.73, f32[]{:T(128)} %get-tuple-element.14, f32[]{:T(128)} %get-tuple-element.15, f32[256]{0:T(256)S(1)} %dynamic_slice.107, f32[512]{0:T(512)S(1)} %dynamic_slice.106, bf16[10240,3,256]{0,2,1:T(8,128)(2,1)S(1)} %copy-done.5, ...), kind=kOutput, calls=%fused_computation.166 | convolution fusion | flops 2685140992 | bytes 16257544 | tf_op jit(solution)/shard_map/dot_general | solution.py:41
  797.5 9.7 %fusion.219 = f32[16,512,256]{2,1,0:T(8,128)} fusion(f32[16,512,256]{2,1,0:T(8,128)} %fusion.214, f32[]{:T(128)} %get-tuple-element.72, f32[]{:T(128)} %get-tuple-element.12, f32[]{:T(128)} %get-tuple-element.13, f32[256]{0:T(256)S(1)} %dynamic_slice.107, f32[512]{0:T(512)S(1)} %dynamic_slice.106, bf16[10240,3,256]{0,2,1:T(8,128)(2,1)S(1)} %copy-done.5, ...), kind=kOutput, calls=%fused_computation.171 | convolution fusion | flops 2685140992 | bytes 16257544 | tf_op jit(solution)/shard_map/dot_general | solution.py:41
  807.2 9.8 %fusion.224 = f32[16,512,256]{2,1,0:T(8,128)} fusion(f32[16,512,256]{2,1,0:T(8,128)} %fusion.219, f32[]{:T(128)} %get-tuple-element.71, f32[]{:T(128)} %get-tuple-element.10, f32[]{:T(128)} %get-tuple-element.11, f32[256]{0:T(256)S(1)} %dynamic_slice.107, f32[512]{0:T(512)S(1)} %dynamic_slice.106, bf16[10240,3,256]{0,2,1:T(8,128)(2,1)S(1)} %copy-done.5, ...), kind=kOutput, calls=%fused_computation.176 | convolution fusion | flops 2685140992 | bytes 16257544 | tf_op jit(solution)/shard_map/dot_general | solution.py:41
  817.0 9.6 %fusion.229 = f32[16,512,256]{2,1,0:T(8,128)} fusion(f32[16,512,256]{2,1,0:T(8,128)} %fusion.224, f32[]{:T(128)} %get-tuple-element.70, f32[]{:T(128)} %get-tuple-element.8, f32[]{:T(128)} %get-tuple-element.9, f32[256]{0:T(256)S(1)} %dynamic_slice.107, f32[512]{0:T(512)S(1)} %dynamic_slice.106, bf16[10240,3,256]{0,2,1:T(8,128)(2,1)S(1)} %copy-done.5, ...), kind=kOutput, calls=%fused_computation.181 | convolution fusion | flops 2685140992 | bytes 16257544 | tf_op jit(solution)/shard_map/dot_general | solution.py:41
  826.6 9.6 %fusion.234 = f32[16,512,256]{2,1,0:T(8,128)} fusion(f32[16,512,256]{2,1,0:T(8,128)} %fusion.229, f32[]{:T(128)} %get-tuple-element.84, f32[]{:T(128)} %get-tuple-element.6, f32[]{:T(128)} %get-tuple-element.7, f32[256]{0:T(256)S(1)} %dynamic_slice.107, f32[512]{0:T(512)S(1)} %dynamic_slice.106, bf16[10240,3,256]{0,2,1:T(8,128)(2,1)S(1)} %copy-done.5, ...), kind=kOutput, calls=%fused_computation.186 | convolution fusion | flops 2685140992 | bytes 16257544 | tf_op jit(solution)/shard_map/dot_general | solution.py:41
  (32 shorter events, 61.8 us)
Async XLA Ops:
  6.5 483.7 %all-gather.5.cloned.1.call-start = ((), (), s32[]{:S(2)}) async-start(), calls=%async_computation.3 | async-start | bytes 19660800 | tf_op jit(solution)/shard_map/all_gather | solution.py:29
  204.3 485.3 %all-gather.3.cloned.1.call-start = ((), (), s32[]{:S(2)}) async-start(), calls=%async_computation.2 | async-start | bytes 35389440 | tf_op jit(solution)/shard_map/all_gather | solution.py:28
  358.1 14.5 %copy-start = (s32[16,2]{0,1:T(2,128)S(1)}, s32[16,2]{0,1:T(2,128)}, u32[]{:S(2)}) copy-start(s32[16,2]{0,1:T(2,128)} %param.11) | copy-start | bytes 388
  358.1 77.3 %copy-start.1 = (s32[16]{0:T(128)S(1)}, s32[16]{0:T(128)}, u32[]{:S(2)}) copy-start(s32[16]{0:T(128)} %param.12) | copy-start | bytes 196
  358.1 78.0 %copy-start.3 = (s32[3]{0:T(128)S(1)}, s32[3]{0:T(128)}, u32[]{:S(2)}) copy-start(s32[3]{0:T(128)} %param.10) | copy-start | bytes 40
  358.1 88.2 %copy-start.2 = (f32[300]{0:T(512)S(1)}, f32[300]{0:T(512)}, u32[]{:S(2)}) copy-start(f32[300]{0:T(512)} %param.8) | copy-start | bytes 3604
  358.1 97.8 %copy-start.4 = (f32[4]{0:T(128)S(1)}, f32[4]{0:T(128)}, u32[]{:S(2)}) copy-start(f32[4]{0:T(128)} %param.13) | copy-start | bytes 52
  689.6 11.8 %copy-start.5 = (bf16[10240,3,256]{0,2,1:T(8,128)(2,1)S(1)}, bf16[10240,3,256]{0,2,1:T(8,128)(2,1)}, u32[]{:S(2)}) copy-start(bf16[10240,3,256]{0,2,1:T(8,128)(2,1)} %all-gather.5.cloned.1.call-done) | copy-start | bytes 47185924
Sparse Core Ops, SparseCore 0:
  204.4 214.8 all-gather.4
  420.9 268.6 all-gather.2
where the time goes:
time: 869 us; the launch traced here: 853 us
  blocking collectives  285 us (33%)
  waiting for transfers between devices  199 us (23%)
  matrix products  156 us (18%)
  local copies, waits for them, and re-layouts  84.6 us (10%)
  between operations  73.8 us (8%)
  other arithmetic  54.2 us (6%)
    all_gather x1, waiting for transfers between devices, shards(): block_a = lax.all_gather(spread_a, 'col', axis=2, tiled=True)  199 us
    dot_general x16, matrix products, shards(): lax.dot_general(left, right, contract, preferred_element_type=jnp.float32)  156 us
    all_to_all x1, blocking collectives, shards(): lax.all_to_all(factors, ('row', 'col'), split_axis=2, concat_axis=0, tile...  143 us
    all_to_all x1, blocking collectives, shards(): lax.all_to_all(reordered, ('row', 'col'), split_axis=2, concat_axis=0, ti...  142 us
    reduce_sum x5, other arithmetic, lookup(): return jnp.sum(jnp.where(hits, table, jnp.zeros_like(table)))  54.2 us
    reshape x1, local copies, waits for them, and re-layouts, shards(): reordered = factors.reshape(local_aux, nocc, n_col, n_row, width).transpo...  31.8 us
  transfers between devices with their start and end apart: 2, of which 1 were waited for; matrix products, arithmetic and copies ran while one was open for 9% of the time, Pallas kernels for 0%

commit v1 on v0

v1 whole, which is shorter than its diff:
```python
import functools

import jax
import jax.numpy as jnp
from jax import lax
from jax.experimental import pallas as pl
from jax.experimental.pallas import tpu as pltpu
from jax.sharding import PartitionSpec as P

MESH = pl.DeviceIdType.MESH
LAG_SOURCE = 1
LAG_RING = 2


def ring_place(row, n_row):
    half = n_row // 2
    return jnp.where(row < half, row, n_row - 1 + half - row)


def gather_kernel(n_row, n_col, x_ref, a_ref, b_ref, recv_a, recv_b, send_row, send_up, send_down, send_pair, send_ring):
    n_chip = n_col // 2
    depth = x_ref.shape[1]
    wide = a_ref.shape[2]
    narrow = b_ref.shape[2]
    row = lax.axis_index("row")
    col = lax.axis_index("col")
    chip = col // 2
    core = col % 2
    has_up = chip + 1 < n_chip
    has_down = chip > 0
    up = (row, lax.rem(col + 2, n_col))
    down = (row, lax.rem(col + n_col - 2, n_col))
    pair = (row, chip * 2 + 1 - core)
    source_row = (col * narrow) // wide
    inside = pl.multiple_of(col * narrow - source_row * wide, narrow)
    place = ring_place(row, n_row)
    hop = lax.rem(place - ring_place(source_row, n_row) + n_row, n_row)
    after = (ring_place(lax.rem(place + 1, n_row), n_row), col)
    before = (ring_place(lax.rem(place + n_row - 1, n_row), n_row), col)

    barrier = pltpu.get_barrier_semaphore()
    for step in range(1, n_row):
        pl.semaphore_signal(barrier, inc=1, device_id=(row ^ step, col), device_id_type=MESH)
    pl.semaphore_signal(barrier, inc=1, device_id=pair, device_id_type=MESH)

    @pl.when(has_up)
    def _():
        pl.semaphore_signal(barrier, inc=1, device_id=up, device_id_type=MESH)

    @pl.when(has_down)
    def _():
        pl.semaphore_signal(barrier, inc=1, device_id=down, device_id_type=MESH)

    pl.semaphore_wait(barrier, n_row + has_up.astype(jnp.int32) + has_down.astype(jnp.int32))

    def a_piece(index):
        return a_ref.at[:, pl.ds(pl.multiple_of(index * depth, depth), depth), :]

    def b_piece(index):
        return b_ref.at[:, pl.ds(pl.multiple_of(index * depth, depth), depth), :]

    def a_columns(index):
        return a_ref.at[:, pl.ds(pl.multiple_of(index * depth, depth), depth), pl.ds(inside, narrow)]

    def x_columns(target):
        return x_ref.at[:, :, pl.ds(pl.multiple_of(target * wide, wide), wide)]

    mine = col * n_row + row

    def row_copy(step):
        return pltpu.make_async_remote_copy(
            src_ref=x_columns(row ^ step), dst_ref=a_piece(mine), send_sem=send_row.at[step],
            recv_sem=recv_a.at[mine], device_id=(row ^ step, col), device_id_type=MESH)

    def line_copy(index, sems, target):
        return pltpu.make_async_remote_copy(
            src_ref=a_piece(index), dst_ref=a_piece(index), send_sem=sems.at[index],
            recv_sem=recv_a.at[index], device_id=target, device_id_type=MESH)

    def ring_copy(source, index, target):
        return pltpu.make_async_remote_copy(
            src_ref=source, dst_ref=b_piece(index), send_sem=send_ring.at[index],
            recv_sem=recv_b.at[index], device_id=target, device_id_type=MESH)

    def own_b_copy(index):
        return pltpu.make_async_copy(a_columns(index), b_piece(index), recv_b.at[index])

    def arrived_a(index):
        pltpu.make_async_copy(a_piece(index), a_piece(index), recv_a.at[index]).wait()

    def arrived_b(index):
        pltpu.make_async_copy(b_piece(index), b_piece(index), recv_b.at[index]).wait()

    pltpu.make_async_copy(x_columns(row), a_piece(mine), recv_a.at[mine]).start()
    for step in range(1, n_row):
        row_copy(step).start()

    total = n_chip * n_row

    def number(chip_at, core_at, step):
        return (chip_at * 2 + core_at) * n_row + (row ^ step)

    def ring_number(chip_at, core_at, step):
        return (chip_at * 2 + core_at) * n_row + (source_row ^ step)

    def each_chip(at, act):
        away = at // n_row
        step = lax.rem(at, n_row)

        @pl.when(away == 0)
        def _():
            act(chip, step, True, True)

        @pl.when((away > 0) & (chip + away < n_chip))
        def _():
            act(chip + away, step, False, True)

        @pl.when((away > 0) & (chip - away >= 0))
        def _():
            act(chip - away, step, True, False)

    def line(chip_at, step, go_up, go_down):
        index = number(chip_at, core, step)
        arrived_a(index)
        if go_up:
            @pl.when(has_up)
            def _():
                line_copy(index, send_up, up).start()
        if go_down:
            @pl.when(has_down)
            def _():
                line_copy(index, send_down, down).start()
        line_copy(index, send_pair, pair).start()

    def line_end(chip_at, step, go_up, go_down):
        index = number(chip_at, core, step)
        if go_up:
            @pl.when(has_up)
            def _():
                line_copy(index, send_up, up).wait_send()
        if go_down:
            @pl.when(has_down)
            def _():
                line_copy(index, send_down, down).wait_send()
        line_copy(index, send_pair, pair).wait_send()

    def source(chip_at, step, go_up, go_down):
        arrived_a(number(chip_at, 1 - core, step))

        @pl.when(hop == 0)
        def _():
            for core_at, target in ((0, after), (1, before)):
                index = number(chip_at, core_at, step)
                ring_copy(a_columns(index), index, target).start()
                own_b_copy(index).start()

    def ring(chip_at, step, go_up, go_down):
        for core_at, target, last in ((0, after, n_row - 1), (1, before, 1)):
            index = ring_number(chip_at, core_at, step)
            arrived_b(index)

            @pl.when((hop != 0) & (hop != last))
            def _():
                ring_copy(b_piece(index), index, target).start()

    def ring_end(chip_at, step, go_up, go_down):
        for core_at, target, last in ((0, after, n_row - 1), (1, before, 1)):
            index = ring_number(chip_at, core_at, step)

            @pl.when(hop != last)
            def _():
                ring_copy(b_piece(index), index, target).wait_send()

    def turn(at, carry):
        @pl.when(at < total)
        def _():
            each_chip(at, line)

        @pl.when((at >= LAG_SOURCE) & (at < total + LAG_SOURCE))
        def _():
            each_chip(at - LAG_SOURCE, source)

        @pl.when(at >= LAG_RING)
        def _():
            each_chip(at - LAG_RING, ring)

        return carry

    lax.fori_loop(0, total + LAG_RING, turn, 0)

    for step in range(1, n_row):
        row_copy(step).wait_send()

    def end(at, carry):
        each_chip(at, line_end)
        each_chip(at, ring_end)
        return carry

    lax.fori_loop(0, total, end, 0)


def gather(x, n_row, n_col):
    nocc, depth, nvir = x.shape
    total = depth * n_row * n_col
    pieces = n_row * n_col
    return pl.pallas_call(
        functools.partial(gather_kernel, n_row, n_col),
        out_shape=(
            jax.ShapeDtypeStruct((nocc, total, nvir // n_row), x.dtype),
            jax.ShapeDtypeStruct((nocc, total, nvir // n_col), x.dtype),
        ),
        in_specs=[pl.BlockSpec(memory_space=pl.ANY)],
        out_specs=(pl.BlockSpec(memory_space=pl.ANY), pl.BlockSpec(memory_space=pl.ANY)),
        scratch_shapes=[
            pltpu.SemaphoreType.DMA((pieces,)),
            pltpu.SemaphoreType.DMA((pieces,)),
            pltpu.SemaphoreType.DMA((n_row,)),
            pltpu.SemaphoreType.DMA((pieces,)),
            pltpu.SemaphoreType.DMA((pieces,)),
            pltpu.SemaphoreType.DMA((pieces,)),
            pltpu.SemaphoreType.DMA((pieces,)),
        ],
        compiler_params=pltpu.CompilerParams(collective_id=0, has_side_effects=True),
        name="gather",
    )(x)


def product_kernel(occ_ref, slab_ref, pair_ref, state_ref, shift_ref, va_ref, vb_ref, a_ref, b_ref, out_ref, acc_ref):
    at = pl.program_id(0)
    nocc = a_ref.shape[0]

    @pl.when(at == 0)
    def _():
        acc_ref[...] = jnp.zeros_like(acc_ref)

    for i in range(nocc):
        left = a_ref[i]
        for j in range(nocc):
            acc_ref[i * nocc + j] += lax.dot_general(
                left, b_ref[j], (((0,), (0,)), ((), ())), preferred_element_type=jnp.float32)

    @pl.when(at == pl.num_programs(0) - 1)
    def _():
        @pl.loop(0, out_ref.shape[0])
        def _(p):
            first = pair_ref[p, 0]
            second = pair_ref[p, 1]
            e_first = occ_ref[slab_ref[first]]
            e_second = occ_ref[slab_ref[second]]
            shift = shift_ref[state_ref[p]]
            denom = (va_ref[...] + vb_ref[...]) - e_first - e_second + shift
            out_ref[p] = -acc_ref[first * nocc + second] / denom


def product(a, b, occ_energy, slab_orbitals, pair_list, pair_state, state_shift, vir_a, vir_b, steps):
    nocc, total, wide = a.shape
    narrow = b.shape[2]
    npair = pair_list.shape[0]
    chunk = total // steps
    smem = pl.BlockSpec(memory_space=pltpu.SMEM)
    return pl.pallas_call(
        product_kernel,
        grid=(steps,),
        out_shape=jax.ShapeDtypeStruct((npair, wide, narrow), jnp.float32),
        in_specs=[smem] * 5 + [
            pl.BlockSpec((wide, 1), lambda s: (0, 0)),
            pl.BlockSpec((1, narrow), lambda s: (0, 0)),
            pl.BlockSpec((nocc, chunk, wide), lambda s: (0, s, 0)),
            pl.BlockSpec((nocc, chunk, narrow), lambda s: (0, s, 0)),
        ],
        out_specs=pl.BlockSpec((npair, wide, narrow), lambda s: (0, 0, 0)),
        scratch_shapes=[pltpu.VMEM((nocc * nocc, wide, narrow), jnp.float32)],
        compiler_params=pltpu.CompilerParams(vmem_limit_bytes=52 * 1024 * 1024),
        name="product",
    )(occ_energy, slab_orbitals, pair_list, pair_state, state_shift, vir_a, vir_b, a, b)


def shards(factors, occ_energy, vir_energy, slab_orbitals, pair_list, pair_state, state_shift):
    n_row = lax.axis_size("row")
    n_col = lax.axis_size("col")
    nvir = factors.shape[2]
    rows_a = nvir // n_row
    cols_b = nvir // n_col
    block_a, block_b = gather(factors.transpose(1, 0, 2), n_row, n_col)
    vir_a = lax.dynamic_slice_in_dim(vir_energy, lax.axis_index("row") * rows_a, rows_a)
    vir_b = lax.dynamic_slice_in_dim(vir_energy, lax.axis_index("col") * cols_b, cols_b)
    return product(block_a, block_b, occ_energy, slab_orbitals, pair_list, pair_state, state_shift,
                   vir_a[:, None], vir_b[None, :], 2 * n_col)


def solution(mesh):
    placed = (P(("row", "col"), None, None), P(), P(), P(), P(), P(), P())
    return jax.shard_map(
        shards, mesh=mesh, in_specs=placed, out_specs=P(None, "row", "col"), check_vma=False
    )
```

time: 869 us -> 743 us (0.86); the launches traced: 853 us -> 742 us
  Pallas kernels: 0 us -> 737 us
  blocking collectives: 285 us -> 0 us
  waiting for transfers between devices: 199 us -> 0 us
  matrix products: 156 us -> 0 us
  local copies, waits for them, and re-layouts: 84.6 us -> 5.06 us
  between operations: 73.8 us -> 0.03 us
  other arithmetic: 54.2 us -> 0 us
    pallas_call x0 -> x2, Pallas kernels: none -> 737 us  [the longest x1 695 us: gather(): pl.pallas_call(functools.partial(gather_kernel, n_row, n_col), out_shape=...]
    all_to_all x2 -> x0, blocking collectives: 285 us -> none  [the longest x1 143 us: shards(): lax.all_to_all(factors, ('row', 'col'), split_axis=2, concat_axis=0, tile...]
    all_gather x2 -> x0, waiting for transfers between devices: 199 us -> none  [the longest x1 199 us: shards(): block_a = lax.all_gather(spread_a, 'col', axis=2, tiled=True)]
    dot_general x16 -> x0, matrix products: 156 us -> none  [shards(): lax.dot_general(left, right, contract, preferred_element_type=jnp.float32)]
    reduce_sum x5 -> x0, other arithmetic: 54.2 us -> none  [lookup(): return jnp.sum(jnp.where(hits, table, jnp.zeros_like(table)))]
    reshape x1 -> x0, local copies, waits for them, and re-layouts: 31.8 us -> none  [shards(): reordered = factors.reshape(local_aux, nocc, n_col, n_row, width).transpo...]
    all_to_all x6 -> x0, local copies, waits for them, and re-layouts: 29.7 us -> none  [the longest x3 15.1 us: shards(): lax.all_to_all(factors, ('row', 'col'), split_axis=2, concat_axis=0, tile...]
    unnamed x14 -> x9, local copies, waits for them, and re-layouts: 16.5 us -> 3.4 us
  transfers between devices with their start and end apart: 2 -> 0, of which waited for: 1 -> 0; matrix products, arithmetic and copies ran while one was open for 9% -> 0% of each run, Pallas kernels for 0% -> 0%
where the time goes in v1:
time: 743 us; the launch traced here: 742 us
  Pallas kernels  737 us (99%)
    pallas_call x1, Pallas kernels, gather(): pl.pallas_call(functools.partial(gather_kernel, n_row, n_col), out_shape=...  695 us
    pallas_call x1, Pallas kernels, product(): pl.pallas_call(product_kernel, grid=(steps,), out_shape=jax.ShapeDtypeStr...  42 us

profile of v1, /device:TPU:28, one launch (start us, length us, event | category | flops | bytes accessed | tf_op | source)
XLA Modules:
  0.0 742.3 jit_solution(3445242430852877258)
XLA Ops:
  0.0 0.8 dynamic_slice.7
  0.8 0.8 dynamic_slice.6
  1.5 0.8 copy.9.pair_ref
  2.3 0.1 copy.10.va_ref
  2.4 695.2 %gather.1 = (bf16[3,10240,512]{2,1,0:T(8,128)(2,1)}, bf16[3,10240,256]{2,1,0:T(8,128)(2,1)}) custom-call(bf16[3,320,2048]{2,1,0:T(8,128)(2,1)} %bitcast.4), custom_call_target="tpu_custom_call" | custom-call | tf_op jit(solution)/shard_map/gather/pallas_call | solution.py:206
  697.6 0.0 copy-start
  697.6 0.7 copy-done
  698.3 0.0 copy-start.1
  698.3 0.7 copy-done.1
  698.9 0.0 copy-start.2
  698.9 0.7 copy-done.2
  699.6 0.0 copy-start.3
  699.6 0.7 copy-done.3
  700.3 42.0 %product.1 = f32[16,512,256]{2,1,0:T(8,128)} custom-call(f32[300]{0:T(512)S(1)} %copy-done, s32[3]{0:T(128)S(1)} %copy-done.1, s32[16,2]{1,0:T(8,128)S(1)} %copy.9.pair_ref, s32[16]{0:T(128)S(1)} %copy-done.2, f32[4]{0:T(128)S(1)} %copy-done.3, f32[512,1]{1,0:T(8,128)S(1)} %copy.10.va_ref, f32[1,256]{1,0:T(1,128)S(1)} %bitcast.3, ...), custom_call_target="tpu_custom_call" | custom-call | tf_op jit(solution)/shard_map/product/pallas_call | solution.py:261
Async XLA Ops:
  697.6 0.7 copy-start
  698.3 0.7 copy-start.1
  698.9 0.7 copy-start.2
  699.6 0.7 copy-start.3

commit v2 on v1

--- a/solution.py
+++ b/solution.py
@@ -9,7 +9,7 @@
 
 MESH = pl.DeviceIdType.MESH
 LAG_SOURCE = 1
-LAG_RING = 2
+LAG_RING = 5
 
 
 def ring_place(row, n_row):

time: 743 us -> 700 us (0.942)
  Pallas kernels: 737 us -> 694 us
    pallas_call x1, Pallas kernels: 695 us -> 652 us  [gather(): pl.pallas_call(functools.partial(gather_kernel, n_row, n_col), out_shape=...]
where the time goes in v2:
time: 700 us; the launch traced here: 699 us
  Pallas kernels  694 us (99%)
    pallas_call x1, Pallas kernels, gather(): pl.pallas_call(functools.partial(gather_kernel, n_row, n_col), out_shape=...  652 us
    pallas_call x1, Pallas kernels, product(): pl.pallas_call(product_kernel, grid=(steps,), out_shape=jax.ShapeDtypeStr...  42 us

profile of v2, /device:TPU:28, one launch (start us, length us, event | category | flops | bytes accessed | tf_op | source)
XLA Modules:
  0.0 699.5 jit_solution(10716686403981293720)
XLA Ops:
  0.0 0.8 dynamic_slice.7
  0.8 0.8 dynamic_slice.6
  1.5 0.8 copy.9.pair_ref
  2.3 0.1 copy.10.va_ref
  2.4 652.4 %gather.1 = (bf16[3,10240,512]{2,1,0:T(8,128)(2,1)}, bf16[3,10240,256]{2,1,0:T(8,128)(2,1)}) custom-call(bf16[3,320,2048]{2,1,0:T(8,128)(2,1)} %bitcast.4), custom_call_target="tpu_custom_call" | custom-call | tf_op jit(solution)/shard_map/gather/pallas_call | solution.py:206
  654.8 0.0 copy-start
  654.8 0.7 copy-done
  655.5 0.0 copy-start.1
  655.5 0.7 copy-done.1
  656.1 0.0 copy-start.2
  656.1 0.7 copy-done.2
  656.8 0.0 copy-start.3
  656.8 0.7 copy-done.3
  657.5 42.0 %product.1 = f32[16,512,256]{2,1,0:T(8,128)} custom-call(f32[300]{0:T(512)S(1)} %copy-done, s32[3]{0:T(128)S(1)} %copy-done.1, s32[16,2]{1,0:T(8,128)S(1)} %copy.9.pair_ref, s32[16]{0:T(128)S(1)} %copy-done.2, f32[4]{0:T(128)S(1)} %copy-done.3, f32[512,1]{1,0:T(8,128)S(1)} %copy.10.va_ref, f32[1,256]{1,0:T(1,128)S(1)} %bitcast.3, ...), custom_call_target="tpu_custom_call" | custom-call | tf_op jit(solution)/shard_map/product/pallas_call | solution.py:261
Async XLA Ops:
  654.8 0.7 copy-start
  655.5 0.7 copy-start.1
  656.1 0.7 copy-start.2
  656.8 0.7 copy-start.3
